TPU v7x, 512 devices: a whole 4x4x16 slice. The times are simulated.
512 devices in a mesh: dp: 32 (over z, core), seq: 16 (over y, x).
Axes of the slice: x: 4, y: 4, z: 16, core: 2. Of those that a mesh axis runs over, the one named last changes fastest.
Arguments:
- features: bfloat16 [262144, 1536], P(('dp', 'seq')), parts along dimension 0, may hold values from -6 to 6
- conv_taps: float32 [5, 1536], replicated, may hold values from -2.5 to 2.5
- norm_gain: float32 [1536], replicated, may hold values from 0.5 to 2
- point_weight: bfloat16 [1536, 1536], replicated, may hold values from -0.15625 to 0.15625
- donor_weight: bfloat16 [1536, 768], replicated, may hold values from -0.15625 to 0.15625
- accept_weight: bfloat16 [1536, 768], replicated, may hold values from -0.15625 to 0.15625
- donor_pos: int32 [32768], P(('dp', 'seq')), parts along dimension 0, may hold values from 0 to 8191, as said below
- accept_pos: int32 [32768], P(('dp', 'seq')), parts along dimension 0, may hold values from 0 to 8191, as said below
- pair_counts: int32 [512], P(('dp', 'seq')), parts along dimension 0, may hold values from 1 to 64, 512 in all
Outputs:
- encoded: bfloat16 [262144, 1536], P(('dp', 'seq')), parts along dimension 0
- junction: bfloat16 [32768, 768], P(('dp', 'seq')), parts along dimension 0
There are 32 independent parts, one for each index of `dp`. A program takes and returns all parts, laid end to end along the dimension named above; an argument that names none is the same for every part. Nothing has to cross between parts.
Inputs may be any that keep to these rules, and one draw needn't show every extreme that they name: `pair_counts`: the live counts sum to 512 and the largest is exactly 64. `donor_pos`: among the 128 donor and acceptor positions of the slots s * 64 to s * 64 + 63, at most 16 lie in any one block of 512 positions r * 512 to r * 512 + 511, and exactly 16 lie in one such block. `accept_pos`: as for donor_pos, with the two lists counted together.
All inputs are finite; a program needn't handle non-finite values. No bound on the sum of `pair_counts` on one device may be relied on, other than what follows from the above.
Results may differ from a plain program's by a relative error of at most 0.0064.
Values may be sent and summed in bfloat16 or wider, within the bound.
A program may use at most 128 MiB of HBM per device.

v0:
```python
import jax
import jax.numpy as jnp
from jax import lax
from jax.sharding import PartitionSpec as P


def padded_2(array, sides, width):
    for axis, dim in sides:
        size, length = (lax.axis_size(axis), array.shape[dim])
        up = [(i, (i + 1) % size) for i in range(size - 1)]
        down = [(j, i) for i, j in up]
        last = lax.slice_in_dim(array, length - width, length, axis=dim)
        leading = lax.slice_in_dim(array, 0, width, axis=dim)
        before = lax.ppermute(last, axis, up)
        after = lax.ppermute(leading, axis, down)
        array = jnp.concatenate([before, array, after], axis=dim)
    return array


def on_device(
    features,
    conv_taps,
    norm_gain,
    point_weight,
    donor_weight,
    accept_weight,
    donor_pos,
    accept_pos,
    pair_counts,
):
    rows = features.shape[0]
    slots = donor_pos.shape[0]
    padded = padded_2(features, (("seq", 0),), 2).astype(jnp.float32)
    conv = conv_taps[0][None, :] * padded[0:rows]
    for k in range(1, conv_taps.shape[0]):
        conv = conv + conv_taps[k][None, :] * padded[k : k + rows]
    scale = lax.rsqrt(jnp.mean(conv * conv, axis=-1, keepdims=True) + 1e-06)
    normed = (conv * scale * norm_gain[None, :]).astype(jnp.bfloat16)
    mixed = jnp.dot(normed, point_weight, preferred_element_type=jnp.float32)
    encoded = (features.astype(jnp.float32) + jax.nn.gelu(mixed, approximate=False)).astype(
        jnp.bfloat16
    )
    wanted = jnp.concatenate([donor_pos, accept_pos])
    piece = lax.all_gather(encoded, "seq", axis=0, tiled=True)
    inside = (wanted >= 0) & (wanted < piece.shape[0])
    taken = jnp.take(piece, jnp.clip(wanted, 0, piece.shape[0] - 1), axis=0)
    picked = jnp.where(inside[:, None], taken.astype(jnp.float32), jnp.float32(0.0)).astype(
        jnp.bfloat16
    )
    donor_rows = picked[:slots]
    accept_rows = picked[slots:]
    live = jnp.arange(slots, dtype=jnp.int32) < pair_counts[0]
    left = jnp.dot(donor_rows, donor_weight, preferred_element_type=jnp.float32)
    right = jnp.dot(accept_rows, accept_weight, preferred_element_type=jnp.float32)
    junction = jnp.where(live[:, None], jax.nn.silu(left) * right, jnp.float32(0.0)).astype(
        jnp.bfloat16
    )
    return (encoded, junction)


def solution(mesh):
    placed = (
        P(("dp", "seq"), None),
        P(),
        P(),
        P(),
        P(),
        P(),
        P(("dp", "seq")),
        P(("dp", "seq")),
        P(("dp", "seq")),
    )
    return jax.shard_map(
        on_device,
        mesh=mesh,
        in_specs=placed,
        out_specs=(P(("dp", "seq"), None), P(("dp", "seq"), None)),
        check_vma=False,
    )
```

profile of v0, /device:TPU:1, one launch (start us, length us, event | category | flops | bytes accessed | tf_op | source)
XLA Modules:
  0.0 231.2 jit_solution(14900449449986693267)
XLA Ops:
  7.2 0.0 copy-start
  7.2 0.0 all-gather.2.cloned.1.call-start
  7.2 0.9 fusion.25
  8.1 3.9 %collective-permute-start = (bf16[2,1536]{1,0:T(2,128)(2,1)S(1)}, bf16[2,1536]{1,0:T(2,128)(2,1)S(1)}, u32[]{:S(2)}, u32[]{:S(2)}) collective-permute-start(bf16[2,1536]{1,0:T(2,128)(2,1)S(1)} %get-tuple-element.9), channel_id=1, source_target_pairs={{0,1},{1,2},{2,3},{3,4},{4,5},{5,6},{6,7},{7,8},{8,9},{9,10},{10,1... | collective-permute-start | bytes 18440 | tf_op jit(solution)/shard_map/ppermute | solution.py:14
  12.1 1.3 collective-permute-start.1
  13.4 1.1 slice_reduce_fusion.4
  14.5 0.0 collective-permute-done
  14.5 2.0 collective-permute-done.1
  16.5 0.0 slice-start
  16.5 2.0 maximum_convert_fusion
  18.5 0.0 copy-start.1
  18.5 0.0 slice-start.1
  18.5 0.0 copy-start.5
  18.5 2.4 %multiply_reduce_fusion = (f32[512]{0:T(512)S(1)}, f32[512,1536]{1,0:T(8,128)S(1)}) fusion(f32[516,1536]{1,0:T(8,128)S(1)} %maximum_convert_fusion, f32[1536]{0:T(1024)S(1)} %get-tuple-element.5, f32[1536]{0:T(1024)S(1)} %get-tuple-element.6, f32[1536]{0:T(1024)S(1)} %get-tuple-element.3, f32[1536]{0:T(1024)S(1)} %get-tuple-element.4, ...), kind=kLoop, calls=%fused_computation.29 | loop fusion | flops 8650240 | bytes 18907136 | tf_op jit(solution)/shard_map/reduce_sum | solution.py:37
  21.0 0.0 slice-done
  21.0 0.0 copy-done.1
  21.0 0.0 slice-done.1
  21.0 0.0 copy-done.5
  21.1 0.0 copy-start.2
  21.1 0.0 copy-start.3
  21.1 10.6 %fusion.3 = bf16[512,1536]{1,0:T(8,128)(2,1)} fusion(bf16[512,1536]{1,0:T(8,128)(2,1)S(1)} %copy-done.1, bf16[1536,1536]{1,0:T(8,128)(2,1)S(1)} %bitcast.12, f32[512,1536]{1,0:T(8,128)S(1)} %get-tuple-element.8, f32[1536]{0:T(1024)S(1)} %copy-done.5, f32[512]{0:T(512)S(1)} %add_rsqrt_fusion), kind=kOutput, calls=%fused_computation.5 | convolution fusion | flops 2470969344 | bytes 11018240 | tf_op jit(solution)/shard_map/dot_general | solution.py:39
  31.7 0.0 all-gather.2.cloned.1.call-update
  32.4 0.0 copy-done.2
  32.4 0.0 copy-done.3
  32.4 0.1 fusion.23
  32.5 0.1 compare_and_fusion.1
  32.6 176.3 %all-gather.2.cloned.1.call-done = bf16[8192,1536]{1,0:T(8,128)(2,1)} async-done(((bf16[512,1536]{1,0:T(8,128)(2,1)}), bf16[8192,1536]{1,0:T(8,128)(2,1)}) %all-gather.2.cloned.1.call-update) | async-done | bytes 25165840 | tf_op jit(solution)/shard_map/all_gather | solution.py:44
  208.8 12.6 %gather_fusion = bf16[128,1536]{1,0:T(8,128)(2,1)S(1)} fusion(bf16[8192,1536]{1,0:T(8,128)(2,1)} %all-gather.2.cloned.1.call-done, s32[1024]{0:T(1024)S(1)} %pad_clamp_fusion), kind=kCustom, calls=%fused_computation | custom fusion | bytes 786944 | tf_op jit(solution)/shard_map/jit(_take)/gather | solution.py:46
  221.5 0.0 copy-start.4
  221.5 0.2 select_convert_fusion
  221.7 0.0 copy-done
  221.7 0.5 fusion.21
  222.2 0.9 copy-done.4
  223.1 1.2 fusion.19
  (4 shorter events, 0.0 us)
Async XLA Ops:
  7.2 214.5 %copy-start = (bf16[1536,768]{1,0:T(8,128)(2,1)S(1)}, bf16[1536,768]{1,0:T(8,128)(2,1)}, u32[]{:S(2)}) copy-start(bf16[1536,768]{1,0:T(8,128)(2,1)} %param.13) | copy-start | bytes 7077892
  7.2 201.6 %all-gather.2.cloned.1.call-start = ((), (), s32[]{:S(2)}) async-start(), calls=%async_computation | async-start | bytes 26738688 | tf_op jit(solution)/shard_map/all_gather | solution.py:44
  8.1 6.3 %collective-permute-start = (bf16[2,1536]{1,0:T(2,128)(2,1)S(1)}, bf16[2,1536]{1,0:T(2,128)(2,1)S(1)}, u32[]{:S(2)}, u32[]{:S(2)}) collective-permute-start(bf16[2,1536]{1,0:T(2,128)(2,1)S(1)} %get-tuple-element.9), channel_id=1, source_target_pairs={{0,1},{1,2},{2,3},{3,4},{4,5},{5,6},{6,7},{7,8},{8,9},{9,10},{10,1... | collective-permute-start | bytes 18440 | tf_op jit(solution)/shard_map/ppermute | solution.py:14
  12.1 4.4 %collective-permute-start.1 = (bf16[2,1536]{1,0:T(2,128)(2,1)S(1)}, bf16[2,1536]{1,0:T(2,128)(2,1)S(1)}, u32[]{:S(2)}, u32[]{:S(2)}) collective-permute-start(bf16[2,1536]{1,0:T(2,128)(2,1)S(1)} %get-tuple-element.10), channel_id=1, source_target_pairs={{1,0},{2,1},{3,2},{4,3},{5,4},{6,5},{7,6},{8,7},{9,8},{10,9},{11,1... | collective-permute-start | bytes 18440 | tf_op jit(solution)/shard_map/ppermute | solution.py:15
  16.5 4.5 %slice-start = ((s8[4718592]{0:T(1024)(128)(4,1)}), s8[4194304]{0:T(1024)(128)(4,1)S(1)}, s32[]{:S(2)}) async-start(s8[4718592]{0:T(1024)(128)(4,1)} %bitcast.11), calls=%async_computation.1 | async-start | bytes 8388608
  18.5 2.5 %copy-start.1 = (bf16[512,1536]{1,0:T(8,128)(2,1)S(1)}, bf16[512,1536]{1,0:T(8,128)(2,1)}, u32[]{:S(2)}) copy-start(bf16[512,1536]{1,0:T(8,128)(2,1)} %param.9) | copy-start | bytes 4718596
  18.5 2.5 %slice-start.1 = ((s8[4718592]{0:T(1024)(128)(4,1)}), s8[524288]{0:T(1024)(128)(4,1)S(1)}, s32[]{:S(2)}) async-start(s8[4718592]{0:T(1024)(128)(4,1)} %bitcast.11), calls=%async_computation.2 | async-start | bytes 1048576
  18.5 2.5 %copy-start.5 = (f32[1536]{0:T(1024)S(1)}, f32[1536]{0:T(1024)}, u32[]{:S(2)}) copy-start(f32[1536]{0:T(1024)} %param.11) | copy-start | bytes 18436
  21.1 11.3 %copy-start.2 = (s32[64]{0:T(128)S(1)}, s32[64]{0:T(128)}, u32[]{:S(2)}) copy-start(s32[64]{0:T(128)} %param.16) | copy-start | bytes 772
  21.1 11.3 %copy-start.3 = (s32[64]{0:T(128)S(1)}, s32[64]{0:T(128)}, u32[]{:S(2)}) copy-start(s32[64]{0:T(128)} %param.15) | copy-start | bytes 772
  221.5 1.7 copy-start.4
Sparse Core Ops, SparseCore 0:
  31.8 176.9 all-gather.1
where the time goes:
time: 231 us
  waiting for transfers between devices  178 us (77%)
  local copies, waits for them, and re-layouts  15.6 us (7%)
  between operations  14.9 us (6%)
  matrix products  12.3 us (5%)
  starting transfers between devices  5.27 us (2%)
  other arithmetic  4.85 us (2%)
    all_gather x1, waiting for transfers between devices, on_device(): piece = lax.all_gather(encoded, 'seq', axis=0, tiled=True)  176 us
    gather x1, local copies, waits for them, and re-layouts, on_device(): taken = jnp.take(piece, jnp.clip(wanted, 0, piece.shape[0] - 1), axis=0)  12.6 us
    dot_general x1, matrix products, on_device(): mixed = jnp.dot(normed, point_weight, preferred_element_type=jnp.float32)  10.6 us
  transfers between devices with their start and end apart: 3, of which 2 were waited for; matrix products, arithmetic and copies ran while one was open for 1% of the time, Pallas kernels for 0%

commit v1 on v0

--- a/solution.py
+++ b/solution.py
@@ -41,7 +41,9 @@
         jnp.bfloat16
     )
     wanted = jnp.concatenate([donor_pos, accept_pos])
-    piece = lax.all_gather(encoded, "seq", axis=0, tiled=True)
+    piece = jnp.concatenate(
+        lax.all_to_all(jnp.stack([encoded] * lax.axis_size("seq")), "seq", 0, 0), axis=0
+    )
     inside = (wanted >= 0) & (wanted < piece.shape[0])
     taken = jnp.take(piece, jnp.clip(wanted, 0, piece.shape[0] - 1), axis=0)
     picked = jnp.where(inside[:, None], taken.astype(jnp.float32), jnp.float32(0.0)).astype(

time: 231 us -> 427 us (1.85)
  waiting for transfers between devices: 178 us -> 368 us
  between operations: 14.9 us -> 1.49 us
  local copies, waits for them, and re-layouts: 15.6 us -> 25.3 us
  starting transfers between devices: 5.27 us -> 13.7 us
    all_to_all x0 -> x1, waiting for transfers between devices: none -> 366 us  [on_device(): lax.all_to_all(jnp.stack([encoded] * lax.axis_size('seq')), 'seq', 0, 0)]
    all_gather x1 -> x0, waiting for transfers between devices: 176 us -> none  [on_device(): piece = lax.all_gather(encoded, 'seq', axis=0, tiled=True)]
    another operation x0 -> x1, local copies, waits for them, and re-layouts: none -> 8.55 us  [on_device(): jnp.stack([encoded] * lax.axis_size('seq'))]
    all_to_all x0 -> x1, starting transfers between devices: none -> 8.49 us  [on_device(): lax.all_to_all(jnp.stack([encoded] * lax.axis_size('seq')), 'seq', 0, 0)]
  transfers between devices with their start and end apart: 3 -> 3, of which waited for: 2 -> 2; matrix products, arithmetic and copies ran while one was open for 1% -> 0% of each run, Pallas kernels for 0% -> 0%
where the time goes in v1:
time: 427 us; the launch traced here: 424 us
  waiting for transfers between devices  368 us (86%)
  local copies, waits for them, and re-layouts  25.3 us (6%)
  starting transfers between devices  13.7 us (3%)
  matrix products  11.3 us (3%)
  other arithmetic  4.85 us (1%)
    all_to_all x1, waiting for transfers between devices, on_device(): lax.all_to_all(jnp.stack([encoded] * lax.axis_size('seq')), 'seq', 0, 0)  366 us
    gather x1, local copies, waits for them, and re-layouts, on_device(): taken = jnp.take(piece, jnp.clip(wanted, 0, piece.shape[0] - 1), axis=0)  12.6 us
    dot_general x1, matrix products, on_device(): mixed = jnp.dot(normed, point_weight, preferred_element_type=jnp.float32)  9.56 us
    another operation x1, local copies, waits for them, and re-layouts, on_device(): jnp.stack([encoded] * lax.axis_size('seq'))  8.55 us
  transfers between devices with their start and end apart: 3, of which 2 were waited for; matrix products, arithmetic and copies ran while one was open for 0% of the time, Pallas kernels for 0%

profile of v1, /device:TPU:1, one launch (start us, length us, event | category | flops | bytes accessed | tf_op | source)
XLA Modules:
  0.0 424.2 jit_solution(2758670879602054566)
XLA Ops:
  0.6 0.0 copy-start
  0.6 0.9 fusion.25
  1.6 3.9 collective-permute-start
  5.5 1.3 collective-permute-start.1
  6.8 1.1 slice_reduce_fusion.4
  7.9 0.0 collective-permute-done
  7.9 2.0 collective-permute-done.1
  9.9 0.0 slice-start
  9.9 2.0 maximum_convert_fusion
  11.9 0.0 copy-start.1
  11.9 0.0 slice-start.1
  11.9 0.0 copy-start.6
  12.0 2.4 multiply_reduce_fusion
  14.4 0.0 slice-done
  14.4 0.0 copy-done.1
  14.4 0.0 slice-done.1
  14.5 0.0 copy-done.6
  14.5 9.6 %fusion.3 = bf16[512,1536]{1,0:T(8,128)(2,1)S(1)} fusion(bf16[512,1536]{1,0:T(8,128)(2,1)S(1)} %copy-done.1, bf16[1536,1536]{1,0:T(8,128)(2,1)S(1)} %bitcast.13, f32[512,1536]{1,0:T(8,128)S(1)} %get-tuple-element.8, f32[1536]{0:T(1024)S(1)} %copy-done.6, f32[512]{0:T(512)S(1)} %add_rsqrt_fusion), kind=kOutput, calls=%fused_computation.5 | convolution fusion | flops 2470969344 | bytes 11018240 | tf_op jit(solution)/shard_map/dot_general | solution.py:39
  24.0 0.0 copy-start.2
  24.1 1.1 copy-done.2
  25.2 8.5 %stack.2 = bf16[16,512,1536]{2,1,0:T(8,128)(2,1)} broadcast(bf16[512,1536]{1,0:T(8,128)(2,1)S(1)} %fusion.3), dimensions={1,2} | broadcast | bytes 26738688 | tf_op jit(solution)/shard_map/stack | solution.py:45
  33.7 0.0 copy-start.3
  33.7 0.0 copy-start.4
  33.7 8.5 %all-to-all-start = ((bf16[16,512,1536]{2,1,0:T(8,128)(2,1)}), bf16[16,512,1536]{2,1,0:T(8,128)(2,1)}, u32[]{:S(2)}, u32[]{:S(2)}) async-start(bf16[16,512,1536]{2,1,0:T(8,128)(2,1)} %stack.2), calls=%async_computation | async-start | bytes 50331648 | tf_op jit(solution)/shard_map/all_to_all | solution.py:45
  42.9 0.0 copy-done.3
  42.9 0.0 copy-done.4
  42.9 0.1 fusion.23
  43.0 0.1 compare_and_fusion.1
  43.1 365.6 %all-to-all-done = bf16[16,512,1536]{2,1,0:T(8,128)(2,1)} async-done(((bf16[16,512,1536]{2,1,0:T(8,128)(2,1)}), bf16[16,512,1536]{2,1,0:T(8,128)(2,1)}, u32[]{:S(2)}, u32[]{:S(2)}) %all-to-all-start) | async-done | bytes 25165856 | tf_op jit(solution)/shard_map/all_to_all | solution.py:45
  408.7 12.6 %gather_fusion = bf16[128,1536]{1,0:T(8,128)(2,1)S(1)} fusion(bf16[8192,1536]{1,0:T(8,128)(2,1)} %bitcast.1, s32[1024]{0:T(1024)S(1)} %pad_clamp_fusion), kind=kCustom, calls=%fused_computation | custom fusion | bytes 786944 | tf_op jit(solution)/shard_map/jit(_take)/gather | solution.py:48
  421.3 0.0 copy-start.5
  421.3 0.2 select_convert_fusion
  421.5 0.0 copy-done
  421.5 0.5 fusion.21
  422.1 0.9 copy-done.5
  423.0 1.2 fusion.19
  (4 shorter events, 0.0 us)
Async XLA Ops:
  0.6 420.9 %copy-start = (bf16[1536,768]{1,0:T(8,128)(2,1)S(1)}, bf16[1536,768]{1,0:T(8,128)(2,1)}, u32[]{:S(2)}) copy-start(bf16[1536,768]{1,0:T(8,128)(2,1)} %param.13) | copy-start | bytes 7077892
  1.6 6.3 %collective-permute-start = (bf16[2,1536]{1,0:T(2,128)(2,1)S(1)}, bf16[2,1536]{1,0:T(2,128)(2,1)S(1)}, u32[]{:S(2)}, u32[]{:S(2)}) collective-permute-start(bf16[2,1536]{1,0:T(2,128)(2,1)S(1)} %get-tuple-element.9), channel_id=1, source_target_pairs={{0,1},{1,2},{2,3},{3,4},{4,5},{5,6},{6,7},{7,8},{8,9},{9,10},{10,1... | collective-permute-start | bytes 18440 | tf_op jit(solution)/shard_map/ppermute | solution.py:14
  5.5 4.4 %collective-permute-start.1 = (bf16[2,1536]{1,0:T(2,128)(2,1)S(1)}, bf16[2,1536]{1,0:T(2,128)(2,1)S(1)}, u32[]{:S(2)}, u32[]{:S(2)}) collective-permute-start(bf16[2,1536]{1,0:T(2,128)(2,1)S(1)} %get-tuple-element.10), channel_id=1, source_target_pairs={{1,0},{2,1},{3,2},{4,3},{5,4},{6,5},{7,6},{8,7},{9,8},{10,9},{11,1... | collective-permute-start | bytes 18440 | tf_op jit(solution)/shard_map/ppermute | solution.py:15
  9.9 4.5 %slice-start = ((s8[4718592]{0:T(1024)(128)(4,1)}), s8[4194304]{0:T(1024)(128)(4,1)S(1)}, s32[]{:S(2)}) async-start(s8[4718592]{0:T(1024)(128)(4,1)} %bitcast.12), calls=%async_computation.1 | async-start | bytes 8388608
  11.9 2.5 copy-start.1
  11.9 2.5 slice-start.1
  11.9 2.5 copy-start.6
  24.0 1.1 copy-start.2
  33.7 9.2 %copy-start.3 = (s32[64]{0:T(128)S(1)}, s32[64]{0:T(128)}, u32[]{:S(2)}) copy-start(s32[64]{0:T(128)} %param.16) | copy-start | bytes 772
  33.7 9.2 %copy-start.4 = (s32[64]{0:T(128)S(1)}, s32[64]{0:T(128)}, u32[]{:S(2)}) copy-start(s32[64]{0:T(128)} %param.15) | copy-start | bytes 772
  33.7 374.9 %all-to-all-start = ((bf16[16,512,1536]{2,1,0:T(8,128)(2,1)}), bf16[16,512,1536]{2,1,0:T(8,128)(2,1)}, u32[]{:S(2)}, u32[]{:S(2)}) async-start(bf16[16,512,1536]{2,1,0:T(8,128)(2,1)} %stack.2), calls=%async_computation | async-start | bytes 50331648 | tf_op jit(solution)/shard_map/all_to_all | solution.py:45
  421.3 1.7 copy-start.5
